TPU v7x, 128 devices: a whole 4x4x4 slice. The times are simulated.
128 devices in a mesh: gx: 8 (over z, core), gy: 16 (over y, x).
Axes of the slice: x: 4, y: 4, z: 4, core: 2. Of those that a mesh axis runs over, the one named last changes fastest.
Arguments:
- displacement: float32 [3, 24, 384, 384], P(None, 'gx', 'gy'), may hold values from -1.6015 to 1.6015, as said below
- velocity: float32 [3, 24, 384, 384], P(None, 'gx', 'gy'), may hold values from -6 to 6
- energy: float32 [27, 8, 128, 128], P(None, 'gx', 'gy'), may hold values from 0.5 to 18
- mass_weight: float32 [216, 8, 128, 128], P(None, 'gx', 'gy'), may hold values from 0.002 to 0.02
- pinned_flags: int32 [3, 24, 384, 384], P(None, 'gx', 'gy'), may hold values 0 or 1
Outputs:
- acceleration: float32 [3, 24, 384, 384], P(None, 'gx', 'gy')
- velocity_new: float32 [3, 24, 384, 384], P(None, 'gx', 'gy')
- displacement_new: float32 [3, 24, 384, 384], P(None, 'gx', 'gy')
- energy_new: float32 [27, 8, 128, 128], P(None, 'gx', 'gy')
Inputs may be any that keep to these rules, and one draw needn't show every extreme that they name: Every entry of the displacement's derivative along local element coordinates stays below 0.11 in magnitude.
All inputs are finite; a program needn't handle non-finite values. No bound on the sum of `pinned_flags` on one device may be relied on, other than what follows from the above.
Results may differ from a plain program's by a relative error of at most 0.00018.
Values sent between devices are 32-bit elements; how exact they have to be, the bound alone decides.
No kernel may reach another device: no remote copies, remote signals or barrier semaphores. Data moves between devices by JAX's collectives and lax.ppermute only.
A program may use at most 128 MiB of HBM per device.

v0:
```python
from functools import partial
import math
import jax
import jax.numpy as jnp
import numpy as np
from jax import lax
from jax.sharding import PartitionSpec as P

Q = 6
ITERS = 3
HIGHEST = lax.Precision.HIGHEST
step_size = 0.05
viscosity = 0.3
gamma_less = 0.4


def shifted_2(shard, axis, by):
    devices = lax.axis_size(axis)
    return lax.ppermute(shard, axis, [(i, (i + by) % devices) for i in range(devices)])


def basis_tables():
    root_five = 1.0 / math.sqrt(5.0)
    lobatto = np.array([0.0, 0.5 - 0.5 * root_five, 0.5 + 0.5 * root_five, 1.0])
    legendre = np.array(
        [
            -0.932469514203152,
            -0.6612093864662645,
            -0.2386191860831909,
            0.2386191860831909,
            0.6612093864662645,
            0.932469514203152,
        ]
    )
    abscissa = 0.5 + 0.5 * legendre
    shape_values = np.ones((6, 4))
    shape_slopes = np.zeros((6, 4))
    for a in range(4):
        for b in range(4):
            if b != a:
                shape_values[:, a] = (
                    shape_values[:, a] * (abscissa - lobatto[b]) / (lobatto[a] - lobatto[b])
                )
        for c in range(4):
            if c != a:
                factor_term = np.ones(6) / (lobatto[a] - lobatto[c])
                for b in range(4):
                    if b != a and b != c:
                        factor_term = (
                            factor_term * (abscissa - lobatto[b]) / (lobatto[a] - lobatto[b])
                        )
                shape_slopes[:, a] = shape_slopes[:, a] + factor_term
    thermo_values = np.stack(
        [
            (1.0 - abscissa) * (1.0 - abscissa),
            2.0 * abscissa * (1.0 - abscissa),
            abscissa * abscissa,
        ],
        axis=1,
    )
    return (
        jnp.asarray(shape_values, jnp.float32),
        jnp.asarray(shape_slopes, jnp.float32),
        jnp.asarray(thermo_values, jnp.float32),
    )


def along_x(matrix, operand):
    return jnp.einsum("qa,cabgjk->cqbgjk", matrix, operand, precision=HIGHEST)


def along_y(matrix, operand):
    return jnp.einsum("qb,cabgjk->caqgjk", matrix, operand, precision=HIGHEST)


def along_z(matrix, operand):
    return jnp.einsum("qg,cabgjk->cabqjk", matrix, operand, precision=HIGHEST)


def split_nodes(operand, which_axis):
    num_cells = (operand.shape[which_axis] - 1) // 3
    outer_dims = operand.shape[:which_axis]
    inner_dims = operand.shape[which_axis + 1 :]
    head_part = lax.slice_in_dim(operand, 0, 3 * num_cells, axis=which_axis).reshape(
        outer_dims + (num_cells, 3) + inner_dims
    )
    head_part = jnp.moveaxis(head_part, which_axis + 1, which_axis)
    tail_part = lax.slice_in_dim(operand, 3, 3 * num_cells + 1, stride=3, axis=which_axis)
    return jnp.concatenate([head_part, jnp.expand_dims(tail_part, which_axis)], axis=which_axis)


def merge_nodes(operand, which_axis):
    num_cells = operand.shape[which_axis + 1]
    outer_dims = operand.shape[:which_axis]
    inner_dims = operand.shape[which_axis + 2 :]
    head_part = jnp.moveaxis(
        lax.slice_in_dim(operand, 0, 3, axis=which_axis), which_axis, which_axis + 1
    )
    head_part = head_part.reshape(outer_dims + (3 * num_cells,) + inner_dims)
    tail_part = jnp.moveaxis(
        lax.slice_in_dim(operand, 3, 4, axis=which_axis), which_axis, which_axis + 1
    )
    pad_tail = [(0, 0)] * tail_part.ndim
    pad_tail[which_axis + 1] = (0, 2)
    tail_part = jnp.pad(tail_part, pad_tail).reshape(outer_dims + (3 * num_cells,) + inner_dims)
    pad_head = [(0, 0)] * head_part.ndim
    pad_head[which_axis] = (0, 1)
    pad_shift = [(0, 0)] * head_part.ndim
    pad_shift[which_axis] = (3, 0)
    shifted = lax.slice_in_dim(jnp.pad(tail_part, pad_shift), 0, 3 * num_cells + 1, axis=which_axis)
    return jnp.pad(head_part, pad_head) + shifted


def slab_elements(slab_field):
    closed = jnp.concatenate([slab_field, slab_field[..., :1]], axis=-1)
    parts_y = split_nodes(closed, 2)
    parts_z = split_nodes(parts_y, 4)
    return jnp.moveaxis(parts_z, 4, 3)


def slab_assemble(element_field):
    parts_z = merge_nodes(jnp.moveaxis(element_field, 3, 4), 4)
    parts_y = merge_nodes(parts_z, 2)
    return jnp.concatenate([parts_y[..., :1] + parts_y[..., -1:], parts_y[..., 1:-1]], axis=-1)


def over_blocks(node_fields, cell_data, element_fn):
    num_cells = cell_data[0].shape[1]

    def one_block(block_index):
        node_start = 3 * block_index
        element_sets = tuple(
            (
                slab_elements(lax.dynamic_slice_in_dim(field_in, node_start, 4, axis=1))
                for field_in in node_fields
            )
        )
        cell_block = tuple(
            (
                lax.dynamic_index_in_dim(member, block_index, axis=1, keepdims=False)
                for member in cell_data
            )
        )
        contribution, outputs_extra = element_fn(element_sets, cell_block)
        return (slab_assemble(contribution), outputs_extra)

    node_pieces, extra_parts = lax.map(one_block, jnp.arange(num_cells, dtype=jnp.int32))
    assembled = merge_nodes(jnp.moveaxis(node_pieces, 0, 2), 1)
    return (assembled, tuple((jnp.moveaxis(member, 0, 1) for member in extra_parts)))


def thermo_interp(thermo_values, dofs):
    return along_x(thermo_values, along_y(thermo_values, along_z(thermo_values, dofs[None])))[0]


def thermo_project(thermo_values, at_quad):
    moved = thermo_values.T
    return along_x(moved, along_y(moved, along_z(moved, at_quad[None])))[0]


def force_block(element_sets, cell_block, basis_set):
    shape_values, shape_slopes, thermo_values = basis_set
    kinematic = element_sets[0]
    energy_block, weight_block = cell_block
    trailing_shape = energy_block.shape[1:]
    z_values = along_z(shape_values, kinematic)
    z_slopes = along_z(shape_slopes, kinematic)
    yz_values = along_y(shape_values, z_values)
    gradients = [
        along_x(shape_slopes, yz_values),
        along_x(shape_values, along_y(shape_slopes, z_values)),
        along_x(shape_values, along_y(shape_values, z_slopes)),
    ]
    jacobian = [[gradients[d][c] + (1.0 if c == d else 0.0) for d in range(3)] for c in range(3)]
    grad_vel = [[gradients[d][3 + c] for d in range(3)] for c in range(3)]
    cofactor = [
        [
            jacobian[(c + 1) % 3][(d + 1) % 3] * jacobian[(c + 2) % 3][(d + 2) % 3]
            - jacobian[(c + 1) % 3][(d + 2) % 3] * jacobian[(c + 2) % 3][(d + 1) % 3]
            for d in range(3)
        ]
        for c in range(3)
    ]
    determinant = (
        jacobian[0][0] * cofactor[0][0]
        + jacobian[0][1] * cofactor[0][1]
        + jacobian[0][2] * cofactor[0][2]
    )
    inverse_det = 1.0 / determinant
    spatial_grad = [
        [
            (
                grad_vel[c][0] * cofactor[e][0]
                + grad_vel[c][1] * cofactor[e][1]
                + grad_vel[c][2] * cofactor[e][2]
            )
            * inverse_det
            for e in range(3)
        ]
        for c in range(3)
    ]
    energy_quad = thermo_interp(thermo_values, energy_block.reshape((3, 3, 3) + trailing_shape))
    mass_quad = weight_block.reshape((Q, Q, Q) + trailing_shape)
    scale_quad = mass_quad * inverse_det
    stress_shape = [
        [
            viscosity * (spatial_grad[c][d] + spatial_grad[d][c])
            - (gamma_less * energy_quad if c == d else 0.0)
            for d in range(3)
        ]
        for c in range(3)
    ]
    flux = [
        [
            scale_quad
            * (
                stress_shape[c][0] * cofactor[0][f]
                + stress_shape[c][1] * cofactor[1][f]
                + stress_shape[c][2] * cofactor[2][f]
            )
            for f in range(3)
        ]
        for c in range(3)
    ]
    power_quad = jnp.zeros_like(mass_quad)
    for c in range(3):
        for f in range(3):
            power_quad = power_quad + flux[c][f] * grad_vel[c][f]
    flux_cols = [jnp.stack([flux[c][f] for c in range(3)]) for f in range(3)]
    moved = along_x(shape_slopes.T, along_y(shape_values.T, along_z(shape_values.T, flux_cols[0])))
    moved = moved + along_x(
        shape_values.T,
        along_y(shape_slopes.T, along_z(shape_values.T, flux_cols[1]))
        + along_y(shape_values.T, along_z(shape_slopes.T, flux_cols[2])),
    )
    energy_rhs = thermo_project(thermo_values, power_quad)
    lumped_mass = thermo_project(thermo_values, mass_quad)
    energy_next = energy_block + step_size * (energy_rhs / lumped_mass).reshape(energy_block.shape)
    return (-moved, (energy_next,))


def mass_block(element_sets, cell_block, basis_set):
    shape_values = basis_set[0]
    mass_quad = cell_block[0].reshape((Q, Q, Q) + cell_block[0].shape[1:])
    at_quad = (
        along_x(shape_values, along_y(shape_values, along_z(shape_values, element_sets[0])))
        * mass_quad
    )
    return (along_x(shape_values.T, along_y(shape_values.T, along_z(shape_values.T, at_quad))), ())


def extend_right(field_in):
    right_rim = shifted_2(field_in[:, :1], "gx", -1)
    wide_field = jnp.concatenate([field_in, right_rim], axis=1)
    top_rim = shifted_2(wide_field[:, :, :1], "gy", -1)
    return jnp.concatenate([wide_field, top_rim], axis=2)


def fold_back(field_in):
    upper_rim = shifted_2(field_in[:, :, -1:], "gy", 1)
    field_in = jnp.concatenate([field_in[:, :, :1] + upper_rim, field_in[:, :, 1:-1]], axis=2)
    side_rim = shifted_2(field_in[:, -1:], "gx", 1)
    return jnp.concatenate([field_in[:, :1] + side_rim, field_in[:, 1:-1]], axis=1)


def global_sum(value):
    return lax.psum(value, ("gx", "gy"))


def on_device(displacement, velocity, energy, mass_weight, pinned_flags):
    basis_set = basis_tables()
    free_mask = (1 - pinned_flags).astype(jnp.float32)
    kinematic = jnp.concatenate([displacement, velocity], axis=0)
    mass_apply = partial(mass_block, basis_set=basis_set)
    rows_x = displacement.shape[1]
    rows_y = displacement.shape[2]
    assembled, extra_parts = over_blocks(
        (extend_right(kinematic),), (energy, mass_weight), partial(force_block, basis_set=basis_set)
    )
    nodal_force = fold_back(assembled)
    owned = 1.0
    residual = free_mask * nodal_force
    energy_new = extra_parts[0]

    def local_inner(first, second):
        return jnp.sum(owned * (first * second))

    acceleration = jnp.zeros_like(residual)
    direction = residual
    norm_now = global_sum(local_inner(residual, residual))
    for iteration in range(ITERS):
        contribution = over_blocks((extend_right(direction),), (mass_weight,), mass_apply)[0]
        mass_image = free_mask * fold_back(contribution)
        step_length = norm_now / global_sum(local_inner(direction, mass_image))
        acceleration = acceleration + step_length * direction
        residual = residual - step_length * mass_image
        norm_next = global_sum(local_inner(residual, residual))
        direction = residual + norm_next / norm_now * direction
        norm_now = norm_next
    acceleration = acceleration[:, :rows_x, :rows_y]
    velocity_new = velocity + step_size * acceleration
    displacement_new = displacement + step_size * velocity_new
    return (acceleration, velocity_new, displacement_new, energy_new)


def solution(mesh):
    in_specs = (
        P(None, "gx", "gy", None),
        P(None, "gx", "gy", None),
        P(None, "gx", "gy", None),
        P(None, "gx", "gy", None),
        P(None, "gx", "gy", None),
    )
    out_specs = (
        P(None, "gx", "gy", None),
        P(None, "gx", "gy", None),
        P(None, "gx", "gy", None),
        P(None, "gx", "gy", None),
    )
    return jax.shard_map(
        on_device, mesh=mesh, in_specs=in_specs, out_specs=out_specs, check_vma=False
    )
```

profile of v0, /device:TPU:1, one launch (start us, length us, event | category | flops | bytes accessed | tf_op | source)
XLA Modules:
  0.0 1001.1 jit_solution(13770269630577380290)
XLA Ops:
  21.4 12.5 %copy.282 = f32[6,4,4,8,384]{3,2,4,1,0:T(4,128)} copy(f32[6,4,4,8,384]{4,3,2,1,0:T(8,128)S(1)} %fusion.109) | data formatting | bytes 2359296 | tf_op jit(solution)/shard_map/while/body/eval_jaxpr/slice | solution.py:84
  33.9 18.3 %copy.283 = f32[6,4,4,8,128,3]{4,5,3,2,1,0:T(4,128)S(1)} copy(f32[6,4,4,8,128,3]{3,2,5,4,1,0:T(4,128)} %bitcast.311) | data formatting | bytes 2359296 | tf_op jit(solution)/shard_map/while/body/eval_jaxpr/reshape | solution.py:84
  52.2 15.2 %slice.434 = f32[6,4,4,8,128]{4,3,2,1,0:T(8,128)S(1)} slice(f32[6,4,4,8,385]{4,3,2,1,0:T(8,128)} %pad_maximum_fusion.3), slice={[0:6:1], [0:4:1], [0:4:1], [0:8:1], [3:385:3]} | slice | bytes 786432 | tf_op jit(solution)/shard_map/while/body/eval_jaxpr/slice | solution.py:88
  86.1 9.3 fusion.18
  101.1 9.5 fusion.16
  110.6 9.5 fusion.20
  121.0 10.7 %copy_bitcast_fusion = (f32[6,6,6,6,8,128]{5,4,3,2,1,0:T(8,128)}, f32[6,6,6,6,8,128]{5,4,3,2,1,0:T(8,128)}) fusion(f32[6,6,6,8,128,6]{4,5,3,2,1,0:T(8,128)} %fusion.16, f32[6,6,6,8,128,6]{4,5,3,2,1,0:T(8,128)} %fusion.18), kind=kLoop, calls=%fused_computation.12 | loop fusion | bytes 21233664 | tf_op jit(solution)/shard_map/while/body/eval_jaxpr/qa,cabgjk->cqbgjk/transpose | solution.py:69
  144.5 11.0 %add_bitcast_fusion = (f32[6,6,6,8,128]{4,3,2,1,0:T(8,128)}, f32[1,6,6,6,8,128]{5,4,3,2,1,0:T(8,128)}, f32[1,6,6,6,8,128]{5,4,3,2,1,0:T(8,128)}, f32[1,6,6,6,8,1...) fusion(f32[1,6,6,6,8,128]{5,4,3,2,1,0:T(8,128)S(1)} %get-tuple-, ...), kind=kLoop, calls=%fused_computation.143 | loop fusion | flops 25878528 | bytes 31850496 | tf_op jit(solution)/shard_map/reshape.83
  184.8 8.2 copy.305
  198.9 10.8 %fusion = f32[3,4,4,8,385]{3,2,4,1,0:T(4,128)} fusion(f32[3,4,4,8,384]{3,2,4,1,0:T(4,128)} %bitcast.323, f32[3,4,4,8,384]{3,2,4,1,0:T(4,128)S(1)} %bitcast.319), kind=kLoop, calls=%fused_computation.4 | loop fusion | flops 147840 | bytes 1771008 | tf_op jit(solution)/shard_map/while/body/eval_jaxpr/add | solution.py:111
  223.7 9.2 copy.307
  262.2 8.0 copy.314
  270.3 10.3 %copy.315 = f32[3,4,4,8,128,3]{4,5,3,2,1,0:T(4,128)} copy(f32[3,4,4,8,128,3]{3,2,5,4,1,0:T(4,128)} %bitcast.327) | data formatting | bytes 1179648 | tf_op jit(solution)/shard_map/while/body/eval_jaxpr/reshape | solution.py:84
  320.0 8.2 copy.322
  328.2 12.8 %fusion.1 = f32[3,4,4,8,385]{3,2,4,1,0:T(4,128)} fusion(f32[3,4,4,8,384]{3,2,4,1,0:T(4,128)} %bitcast.320, f32[3,4,4,8,384]{3,2,4,1,0:T(4,128)} %bitcast.324), kind=kLoop, calls=%fused_computation.5 | loop fusion | flops 147840 | bytes 1771008 | tf_op jit(solution)/shard_map/while/body/eval_jaxpr/add | solution.py:111
  356.5 10.0 copy.324
  388.2 66.0 %all-reduce.36 = (f32[]{:T(128)}, f32[]{:T(128)}) all-reduce(f32[]{:T(128)} %get-tuple-element.88, f32[]{:T(128)} %get-tuple-element.87), channel_id=1, replica_groups=mesh['gx'=8,'gy'=16] {'gx','gy'}, use_global_device_ids=true, to_apply=%region_1.2 | all-reduce | flops 2 | bytes 16 | tf_op jit(solution)/shard_map/psum | solution.py:267
  457.2 62.5 %psum.44 = f32[]{:T(128)} all-reduce(f32[]{:T(128)} %get-tuple-element.114), channel_id=1, replica_groups=mesh['gx'=8,'gy'=16] {'gx','gy'}, use_global_device_ids=true, to_apply=%region_5.6 | all-reduce | flops 1 | bytes 8 | tf_op jit(solution)/shard_map/psum | solution.py:267
  536.6 8.0 copy.332
  544.6 10.3 %copy.333 = f32[3,4,4,8,128,3]{4,5,3,2,1,0:T(4,128)} copy(f32[3,4,4,8,128,3]{3,2,5,4,1,0:T(4,128)} %bitcast.328) | data formatting | bytes 1179648 | tf_op jit(solution)/shard_map/while/body/eval_jaxpr/reshape | solution.py:84
  554.9 8.5 slice.502
  596.9 8.2 copy.339
  605.0 12.8 %fusion.2 = f32[3,4,4,8,385]{3,2,4,1,0:T(4,128)} fusion(f32[3,4,4,8,384]{3,2,4,1,0:T(4,128)} %bitcast.321, f32[3,4,4,8,384]{3,2,4,1,0:T(4,128)} %bitcast.325), kind=kLoop, calls=%fused_computation.6 | loop fusion | flops 147840 | bytes 1771008 | tf_op jit(solution)/shard_map/while/body/eval_jaxpr/add | solution.py:111
  633.3 10.0 copy.341
  665.9 65.0 %psum.45 = f32[]{:T(128)} all-reduce(f32[]{:T(128)} %get-tuple-element.112), channel_id=1, replica_groups=mesh['gx'=8,'gy'=16] {'gx','gy'}, use_global_device_ids=true, to_apply=%region_7.8 | all-reduce | flops 1 | bytes 8 | tf_op jit(solution)/shard_map/psum | solution.py:267
  735.6 62.5 %psum.46 = f32[]{:T(128)} all-reduce(f32[]{:T(128)} %multiply_reduce_fusion), channel_id=1, replica_groups=mesh['gx'=8,'gy'=16] {'gx','gy'}, use_global_device_ids=true, to_apply=%region_9.10 | all-reduce | flops 1 | bytes 8 | tf_op jit(solution)/shard_map/psum | solution.py:267
  813.1 8.0 copy.349
  821.2 10.3 %copy.350 = f32[3,4,4,8,128,3]{4,5,3,2,1,0:T(4,128)} copy(f32[3,4,4,8,128,3]{3,2,5,4,1,0:T(4,128)} %bitcast.329) | data formatting | bytes 1179648 | tf_op jit(solution)/shard_map/while/body/eval_jaxpr/reshape | solution.py:84
  831.5 7.9 slice.527
  877.1 12.9 %fusion.3 = f32[3,4,4,8,385]{3,2,4,1,0:T(4,128)} fusion(f32[3,4,4,8,384]{3,2,4,1,0:T(4,128)} %bitcast.322, f32[3,4,4,8,384]{3,2,4,1,0:T(4,128)} %bitcast.326), kind=kLoop, calls=%fused_computation.7 | loop fusion | flops 147840 | bytes 1771008 | tf_op jit(solution)/shard_map/while/body/eval_jaxpr/add | solution.py:111
  905.4 9.1 copy.358
  933.3 65.1 %psum.47 = f32[]{:T(128)} all-reduce(f32[]{:T(128)} %fusion.140), channel_id=1, replica_groups=mesh['gx'=8,'gy'=16] {'gx','gy'}, use_global_device_ids=true, to_apply=%region_11.12 | all-reduce | flops 1 | bytes 8 | tf_op jit(solution)/shard_map/psum | solution.py:267
  (285 shorter events, 391.5 us)
Async XLA Ops:
  0.6 13.7 %copy-start.25 = (f32[6,3,1,1,1]{0,1,4,3,2:T(4,128)S(1)}, f32[6,3,1,1,1]{0,1,4,3,2:T(4,128)}, u32[]{:S(2)}) copy-start(f32[6,3,1,1,1]{0,1,4,3,2:T(4,128)} %constant.174) | copy-start | bytes 220
  2.7 6.7 collective-permute-start
  9.4 6.4 collective-permute-start.1
  33.9 33.5 %copy-start.18 = (f32[6,4,1,1,1,1]{0,1,5,4,3,2:T(4,128)S(1)}, f32[6,4,1,1,1,1]{0,1,5,4,3,2:T(4,128)}, u32[]{:S(2)}) copy-start(f32[6,4,1,1,1,1]{0,1,5,4,3,2:T(4,128)} %constant.172) | copy-start | bytes 292
  131.7 5.6 slice-start
  131.7 7.5 slice-start.2
  131.7 7.7 slice-start.1
  131.7 8.0 slice-start.3
  139.7 4.8 copy-start.1
  192.9 6.0 copy-start
  235.7 10.8 %copy-start.3 = (s32[3,3,24,384]{3,2,1,0:T(8,128)S(1)}, s32[3,3,24,384]{3,2,1,0:T(8,128)}, u32[]{:S(2)}) copy-start(s32[3,3,24,384]{3,2,1,0:T(8,128)} %param.12) | copy-start | bytes 995332
  235.8 18.2 %copy-start.2 = (f32[216,1,8,128]{3,2,1,0:T(8,128)S(1)}, f32[216,1,8,128]{3,2,1,0:T(8,128)}, u32[]{:S(2)}) copy-start(f32[216,1,8,128]{3,2,1,0:T(8,128)} %param.11) | copy-start | bytes 2654212
  235.8 6.0 collective-permute-start.2
  241.9 4.6 collective-permute-start.3
  246.6 5.5 collective-permute-start.4
  252.2 2.7 collective-permute-start.5
  376.8 6.3 collective-permute-start.6
  383.1 4.2 collective-permute-start.7
  387.4 66.8 %copy-start.22 = (f32[3,1,24,384]{3,2,1,0:T(8,128)}, f32[3,1,24,384]{3,2,1,0:T(8,128)S(1)}, u32[]{:S(2)}) copy-start(f32[3,1,24,384]{3,2,1,0:T(8,128)S(1)} %maximum_add_fusion.2) | copy-start | bytes 331780
  521.1 4.2 collective-permute-start.8
  525.3 3.2 collective-permute-start.9
  654.5 8.6 copy-start.26
  654.9 6.7 collective-permute-start.10
  661.7 3.5 collective-permute-start.11
  799.5 4.2 collective-permute-start.12
  803.7 3.9 collective-permute-start.13
  922.2 8.0 copy-start.24
  922.4 6.0 collective-permute-start.14
  923.4 9.2 copy-start.23
  923.4 76.3 %copy-start.19 = (f32[3,3,24,384]{3,2,1,0:T(8,128)S(1)}, f32[3,3,24,384]{3,2,1,0:T(8,128)}, u32[]{:S(2)}) copy-start(f32[3,3,24,384]{3,2,1,0:T(8,128)} %param.8) | copy-start | bytes 995332
  923.4 76.3 %copy-start.20 = (f32[3,3,24,384]{3,2,1,0:T(8,128)S(1)}, f32[3,3,24,384]{3,2,1,0:T(8,128)}, u32[]{:S(2)}) copy-start(f32[3,3,24,384]{3,2,1,0:T(8,128)} %param.9) | copy-start | bytes 995332
  928.4 3.5 collective-permute-start.15
  (16 other events, 34.7 us)
where the time goes:
time: 1010 us; the launch traced here: 1000 us
  local copies, waits for them, and re-layouts  364 us (36%)
  blocking collectives  321 us (32%)
  matrix products  153 us (15%)
  other arithmetic  88.8 us (9%)
  waiting for transfers between devices  40 us (4%)
  starting transfers between devices  25.2 us (2%)
    psum x5, blocking collectives, global_sum(): return lax.psum(value, ('gx', 'gy'))  321 us
    transpose x16, local copies, waits for them, and re-layouts, merge_nodes(): jnp.moveaxis(lax.slice_in_dim(operand, 0, 3, axis=which_axis), which_axis...  104 us
    dot_general x14, matrix products, along_x(): return jnp.einsum('qa,cabgjk->cqbgjk', matrix, operand, precision=HIGHEST)  55.3 us
    dot_general x15, matrix products, along_y(): return jnp.einsum('qb,cabgjk->caqgjk', matrix, operand, precision=HIGHEST)  50.4 us
    reshape x8, local copies, waits for them, and re-layouts, split_nodes(): lax.slice_in_dim(operand, 0, 3 * num_cells, axis=which_axis)  50.1 us
    add x12, other arithmetic, merge_nodes(): return jnp.pad(head_part, pad_head) + shifted  50 us
    dot_general x14, matrix products, along_z(): return jnp.einsum('qg,cabgjk->cabqjk', matrix, operand, precision=HIGHEST)  47.1 us
    slice x8, local copies, waits for them, and re-layouts, split_nodes(): lax.slice_in_dim(operand, 3, 3 * num_cells + 1, stride=3, axis=which_axis)  46.5 us
  transfers between devices with their start and end apart: 16, of which 13 were waited for; matrix products, arithmetic and copies ran while one was open for 1% of the time, Pallas kernels for 0%

commit v1 on v0

--- a/solution.py
+++ b/solution.py
@@ -264,7 +264,7 @@
 
 
 def global_sum(value):
-    return lax.psum(value, ("gx", "gy"))
+    return lax.psum(lax.psum(value, axis_name="gx"), axis_name="gy")
 
 
 def on_device(displacement, velocity, energy, mass_weight, pinned_flags):

time: 1010 us -> 958 us (0.949)
  blocking collectives: 321 us -> 242 us
  starting transfers between devices: 25.2 us -> 37.1 us
    psum x5 -> x10, blocking collectives: 321 us -> 242 us  [global_sum(): return lax.psum(lax.psum(value, axis_name='gx'), axis_name='gy')]
    ppermute x16, starting transfers between devices: 25.2 us -> 37.1 us  [shifted_2(): lax.ppermute(shard, axis, [(i, (i + by) % devices) for i in range(devices)])]
    unnamed x73 -> x81, local copies, waits for them, and re-layouts: 39.7 us -> 42.1 us
where the time goes in v1:
time: 958 us; the launch traced here: 939 us
  local copies, waits for them, and re-layouts  366 us (38%)
  blocking collectives  242 us (25%)
  matrix products  154 us (16%)
  other arithmetic  92.9 us (10%)
  waiting for transfers between devices  38.5 us (4%)
  starting transfers between devices  37.1 us (4%)
    psum x10, blocking collectives, global_sum(): return lax.psum(lax.psum(value, axis_name='gx'), axis_name='gy')  242 us
    transpose x16, local copies, waits for them, and re-layouts, merge_nodes(): jnp.moveaxis(lax.slice_in_dim(operand, 0, 3, axis=which_axis), which_axis...  102 us
    dot_general x14, matrix products, along_x(): return jnp.einsum('qa,cabgjk->cqbgjk', matrix, operand, precision=HIGHEST)  56.4 us
    dot_general x15, matrix products, along_y(): return jnp.einsum('qb,cabgjk->caqgjk', matrix, operand, precision=HIGHEST)  50.7 us
    reshape x8, local copies, waits for them, and re-layouts, split_nodes(): lax.slice_in_dim(operand, 0, 3 * num_cells, axis=which_axis)  50.1 us
    add x12, other arithmetic, merge_nodes(): return jnp.pad(head_part, pad_head) + shifted  49.9 us
    dot_general x14, matrix products, along_z(): return jnp.einsum('qg,cabgjk->cabqjk', matrix, operand, precision=HIGHEST)  47.3 us
    slice x8, local copies, waits for them, and re-layouts, split_nodes(): lax.slice_in_dim(operand, 3, 3 * num_cells + 1, stride=3, axis=which_axis)  46 us
  transfers between devices with their start and end apart: 16, of which 13 were waited for; matrix products, arithmetic and copies ran while one was open for 1% of the time, Pallas kernels for 0%

profile of v1, /device:TPU:1, one launch (start us, length us, event | category | flops | bytes accessed | tf_op | source)
XLA Modules:
  0.0 939.2 jit_solution(8791267213750315366)
XLA Ops:
  20.2 12.5 %copy.282 = f32[6,4,4,8,384]{3,2,4,1,0:T(4,128)} copy(f32[6,4,4,8,384]{4,3,2,1,0:T(8,128)S(1)} %fusion.109) | data formatting | bytes 2359296 | tf_op jit(solution)/shard_map/while/body/eval_jaxpr/slice | solution.py:84
  32.7 18.3 %copy.283 = f32[6,4,4,8,128,3]{4,5,3,2,1,0:T(4,128)S(1)} copy(f32[6,4,4,8,128,3]{3,2,5,4,1,0:T(4,128)} %bitcast.311) | data formatting | bytes 2359296 | tf_op jit(solution)/shard_map/while/body/eval_jaxpr/reshape | solution.py:84
  51.0 15.0 %slice.434 = f32[6,4,4,8,128]{4,3,2,1,0:T(8,128)S(1)} slice(f32[6,4,4,8,385]{4,3,2,1,0:T(8,128)} %pad_maximum_fusion.3), slice={[0:6:1], [0:4:1], [0:4:1], [0:8:1], [3:385:3]} | slice | bytes 786432 | tf_op jit(solution)/shard_map/while/body/eval_jaxpr/slice | solution.py:88
  85.0 9.3 fusion.18
  100.0 9.4 %fusion.16 = f32[6,6,6,8,128,6]{4,5,3,2,1,0:T(8,128)} fusion(f32[6,4,1,1,1,1]{0,1,5,4,3,2:T(4,128)S(1)} %copy-done.22, f32[6,4,6,6,8,128]{5,2,4,3,1,0:T(8,128)S(1)} %fusion.36), kind=kOutput, calls=%fused_computation.30 | convolution fusion | flops 63700992 | bytes 8847456 | tf_op jit(solution)/shard_map/while/body/eval_jaxpr/qa,cabgjk->cqbgjk/dot_general | solution.py:69
  109.4 9.5 %fusion.20 = f32[6,6,6,8,128,6]{4,5,3,2,1,0:T(8,128)S(1)} fusion(f32[6,4,1,1,1,1]{0,1,5,4,3,2:T(4,128)S(1)} %copy-done.31, f32[6,4,6,6,8,128]{5,2,4,3,1,0:T(8,128)S(1)} %convolution_bitcast_fusion.1), kind=kOutput, calls=%fused_computation.34 | convolution fusion | flops 63700992 | bytes 8847456 | tf_op jit(solution)/shard_map/while/body/eval_jaxpr/qa,cabgjk->cqbgjk/dot_general | solution.py:69
  119.8 10.7 %copy_bitcast_fusion = (f32[6,6,6,6,8,128]{5,4,3,2,1,0:T(8,128)}, f32[6,6,6,6,8,128]{5,4,3,2,1,0:T(8,128)}) fusion(f32[6,6,6,8,128,6]{4,5,3,2,1,0:T(8,128)} %fusion.16, f32[6,6,6,8,128,6]{4,5,3,2,1,0:T(8,128)} %fusion.18), kind=kLoop, calls=%fused_computation.12 | loop fusion | bytes 21233664 | tf_op jit(solution)/shard_map/while/body/eval_jaxpr/qa,cabgjk->cqbgjk/transpose | solution.py:69
  144.1 11.7 %add_bitcast_fusion = (f32[6,6,6,8,128]{4,3,2,1,0:T(8,128)}, f32[1,6,6,6,8,128]{5,4,3,2,1,0:T(8,128)}, f32[1,6,6,6,8,128]{5,4,3,2,1,0:T(8,128)}, f32[1,6,6,6,8,1...) fusion(f32[1,6,6,6,8,128]{5,4,3,2,1,0:T(8,128)} %get-tuple-elem, ...), kind=kLoop, calls=%fused_computation.143 | loop fusion | flops 25878528 | bytes 31850496 | tf_op jit(solution)/shard_map/reshape.83
  200.5 10.8 %fusion = f32[3,4,4,8,385]{3,2,4,1,0:T(4,128)} fusion(f32[3,4,4,8,384]{3,2,4,1,0:T(4,128)} %bitcast.323, f32[3,4,4,8,384]{3,2,4,1,0:T(4,128)S(1)} %bitcast.319), kind=kLoop, calls=%fused_computation.4 | loop fusion | flops 147840 | bytes 1771008 | tf_op jit(solution)/shard_map/while/body/eval_jaxpr/add | solution.py:111
  225.3 9.2 copy.307
  272.9 10.3 %copy.315 = f32[3,4,4,8,128,3]{4,5,3,2,1,0:T(4,128)} copy(f32[3,4,4,8,128,3]{3,2,5,4,1,0:T(4,128)} %bitcast.327) | data formatting | bytes 1179648 | tf_op jit(solution)/shard_map/while/body/eval_jaxpr/reshape | solution.py:84
  322.6 8.3 copy.322
  331.0 12.8 %fusion.1 = f32[3,4,4,8,385]{3,2,4,1,0:T(4,128)} fusion(f32[3,4,4,8,384]{3,2,4,1,0:T(4,128)} %bitcast.320, f32[3,4,4,8,384]{3,2,4,1,0:T(4,128)} %bitcast.324), kind=kLoop, calls=%fused_computation.5 | loop fusion | flops 147840 | bytes 1771008 | tf_op jit(solution)/shard_map/while/body/eval_jaxpr/add | solution.py:111
  359.3 10.0 %copy.324 = f32[3,4,8,3,385]{4,1,3,2,0:T(4,128)} copy(f32[3,4,8,3,385]{2,3,4,1,0:T(4,128)} %slice_bitcast_fusion.2) | data formatting | bytes 887040 | tf_op jit(solution)/shard_map/while/body/eval_jaxpr/transpose | solution.py:96
  391.0 17.0 %all-reduce.37 = (f32[]{:T(128)}, f32[]{:T(128)}) all-reduce(f32[]{:T(128)} %get-tuple-element.88, f32[]{:T(128)} %get-tuple-element.87), channel_id=1, replica_groups=mesh['gx'=8,'gy'=16] {'gx'}, use_global_device_ids=true, to_apply=%region_1.2 | all-reduce | flops 2 | bytes 16 | tf_op jit(solution)/shard_map/psum | solution.py:267
  408.0 30.4 %all-reduce.36 = (f32[]{:T(128)}, f32[]{:T(128)}) all-reduce(f32[]{:T(128)} %get-tuple-element.96, f32[]{:T(128)} %get-tuple-element.97), channel_id=1, replica_groups=mesh['gx'=8,'gy'=16] {'gy'}, use_global_device_ids=true, to_apply=%region_2.3 | all-reduce | flops 2 | bytes 16 | tf_op jit(solution)/shard_map/psum | solution.py:267
  441.3 20.2 %psum.88 = f32[]{:T(128)} all-reduce(f32[]{:T(128)} %get-tuple-element.116), channel_id=1, replica_groups=mesh['gx'=8,'gy'=16] {'gx'}, use_global_device_ids=true, to_apply=%region_7.8 | all-reduce | flops 1 | bytes 8 | tf_op jit(solution)/shard_map/psum | solution.py:267
  461.5 29.5 %psum.89 = f32[]{:T(128)} all-reduce(f32[]{:T(128)} %psum.88), channel_id=1, replica_groups=mesh['gx'=8,'gy'=16] {'gy'}, use_global_device_ids=true, to_apply=%region_8.9 | all-reduce | flops 1 | bytes 8 | tf_op jit(solution)/shard_map/psum | solution.py:267
  520.0 10.3 %copy.333 = f32[3,4,4,8,128,3]{4,5,3,2,1,0:T(4,128)} copy(f32[3,4,4,8,128,3]{3,2,5,4,1,0:T(4,128)} %bitcast.328) | data formatting | bytes 1179648 | tf_op jit(solution)/shard_map/while/body/eval_jaxpr/reshape | solution.py:84
  530.2 8.5 slice.502
  572.1 8.3 copy.339
  580.4 12.8 %fusion.2 = f32[3,4,4,8,385]{3,2,4,1,0:T(4,128)} fusion(f32[3,4,4,8,384]{3,2,4,1,0:T(4,128)} %bitcast.321, f32[3,4,4,8,384]{3,2,4,1,0:T(4,128)} %bitcast.325), kind=kLoop, calls=%fused_computation.6 | loop fusion | flops 147840 | bytes 1771008 | tf_op jit(solution)/shard_map/while/body/eval_jaxpr/add | solution.py:111
  608.7 10.0 %copy.341 = f32[3,4,8,3,385]{4,1,3,2,0:T(4,128)} copy(f32[3,4,8,3,385]{2,3,4,1,0:T(4,128)} %slice_bitcast_fusion.1) | data formatting | bytes 887040 | tf_op jit(solution)/shard_map/while/body/eval_jaxpr/transpose | solution.py:96
  642.3 17.0 %psum.90 = f32[]{:T(128)} all-reduce(f32[]{:T(128)} %get-tuple-element.114), channel_id=1, replica_groups=mesh['gx'=8,'gy'=16] {'gx'}, use_global_device_ids=true, to_apply=%region_10.11 | all-reduce | flops 1 | bytes 8 | tf_op jit(solution)/shard_map/psum | solution.py:267
  659.3 30.4 %psum.91 = f32[]{:T(128)} all-reduce(f32[]{:T(128)} %psum.90), channel_id=1, replica_groups=mesh['gx'=8,'gy'=16] {'gy'}, use_global_device_ids=true, to_apply=%region_11.12 | all-reduce | flops 1 | bytes 8 | tf_op jit(solution)/shard_map/psum | solution.py:267
  694.7 20.2 %psum.92 = f32[]{:T(128)} all-reduce(f32[]{:T(128)} %multiply_reduce_fusion), channel_id=1, replica_groups=mesh['gx'=8,'gy'=16] {'gx'}, use_global_device_ids=true, to_apply=%region_13.14 | all-reduce | flops 1 | bytes 8 | tf_op jit(solution)/shard_map/psum | solution.py:267
  717.6 29.5 %psum.93 = f32[]{:T(128)} all-reduce(f32[]{:T(128)} %psum.92), channel_id=1, replica_groups=mesh['gx'=8,'gy'=16] {'gy'}, use_global_device_ids=true, to_apply=%region_14.15 | all-reduce | flops 1 | bytes 8 | tf_op jit(solution)/shard_map/psum | solution.py:267
  776.1 10.3 %copy.350 = f32[3,4,4,8,128,3]{4,5,3,2,1,0:T(4,128)} copy(f32[3,4,4,8,128,3]{3,2,5,4,1,0:T(4,128)} %bitcast.329) | data formatting | bytes 1179648 | tf_op jit(solution)/shard_map/while/body/eval_jaxpr/reshape | solution.py:84
  832.0 12.8 %fusion.3 = f32[3,4,4,8,385]{3,2,4,1,0:T(4,128)} fusion(f32[3,4,4,8,384]{3,2,4,1,0:T(4,128)} %bitcast.322, f32[3,4,4,8,384]{3,2,4,1,0:T(4,128)} %bitcast.326), kind=kLoop, calls=%fused_computation.7 | loop fusion | flops 147840 | bytes 1771008 | tf_op jit(solution)/shard_map/while/body/eval_jaxpr/add | solution.py:111
  860.3 9.1 copy.358
  888.5 17.0 %psum.94 = f32[]{:T(128)} all-reduce(f32[]{:T(128)} %fusion.140), channel_id=1, replica_groups=mesh['gx'=8,'gy'=16] {'gx'}, use_global_device_ids=true, to_apply=%region_16.17 | all-reduce | flops 1 | bytes 8 | tf_op jit(solution)/shard_map/psum | solution.py:267
  906.2 30.4 %psum.95 = f32[]{:T(128)} all-reduce(f32[]{:T(128)} %psum.94), channel_id=1, replica_groups=mesh['gx'=8,'gy'=16] {'gy'}, use_global_device_ids=true, to_apply=%region_17.18 | all-reduce | flops 1 | bytes 8 | tf_op jit(solution)/shard_map/psum | solution.py:267
  (298 shorter events, 448.9 us)
Async XLA Ops:
  0.6 13.7 %copy-start.29 = (f32[6,3,1,1,1]{0,1,4,3,2:T(4,128)S(1)}, f32[6,3,1,1,1]{0,1,4,3,2:T(4,128)}, u32[]{:S(2)}) copy-start(f32[6,3,1,1,1]{0,1,4,3,2:T(4,128)} %constant.174) | copy-start | bytes 220
  2.7 6.7 collective-permute-start
  9.4 7.5 collective-permute-start.1
  32.7 33.3 %copy-start.22 = (f32[6,4,1,1,1,1]{0,1,5,4,3,2:T(4,128)S(1)}, f32[6,4,1,1,1,1]{0,1,5,4,3,2:T(4,128)}, u32[]{:S(2)}) copy-start(f32[6,4,1,1,1,1]{0,1,5,4,3,2:T(4,128)} %constant.172) | copy-start | bytes 292
  130.6 5.9 slice-start
  130.6 7.8 slice-start.2
  130.6 8.0 slice-start.1
  130.6 8.3 slice-start.3
  144.1 11.7 %copy-start.5 = (f32[1,6,6,6,8,128]{5,4,3,2,1,0:T(8,128)S(1)}, f32[1,6,6,6,8,128]{5,4,3,2,1,0:T(8,128)}, u32[]{:S(2)}) copy-start(f32[1,6,6,6,8,128]{5,4,3,2,1,0:T(8,128)} %get-tuple-element.127) | copy-start | bytes 2654212
  192.8 7.7 copy-start
  238.9 10.3 %copy-start.4 = (s32[3,3,24,384]{3,2,1,0:T(8,128)S(1)}, s32[3,3,24,384]{3,2,1,0:T(8,128)}, u32[]{:S(2)}) copy-start(s32[3,3,24,384]{3,2,1,0:T(8,128)} %param.12) | copy-start | bytes 995332
  239.0 17.1 %copy-start.3 = (f32[216,1,8,128]{3,2,1,0:T(8,128)S(1)}, f32[216,1,8,128]{3,2,1,0:T(8,128)}, u32[]{:S(2)}) copy-start(f32[216,1,8,128]{3,2,1,0:T(8,128)} %param.11) | copy-start | bytes 2654212
  239.0 6.0 collective-permute-start.2
  245.1 4.1 collective-permute-start.3
  249.2 5.5 collective-permute-start.4
  254.8 2.7 collective-permute-start.5
  379.6 6.0 collective-permute-start.6
  385.7 4.5 collective-permute-start.7
  390.2 48.1 %copy-start.26 = (f32[3,1,24,384]{3,2,1,0:T(8,128)}, f32[3,1,24,384]{3,2,1,0:T(8,128)S(1)}, u32[]{:S(2)}) copy-start(f32[3,1,24,384]{3,2,1,0:T(8,128)S(1)} %maximum_add_fusion.2) | copy-start | bytes 331780
  492.5 8.7 collective-permute-start.8
  501.2 2.7 collective-permute-start.9
  630.3 62.4 %copy-start.30 = (f32[6,3,1,1,1]{0,1,4,3,2:T(4,128)S(1)}, f32[6,3,1,1,1]{0,1,4,3,2:T(4,128)}, u32[]{:S(2)}) copy-start(f32[6,3,1,1,1]{0,1,4,3,2:T(4,128)} %constant.174) | copy-start | bytes 220
  630.3 6.0 collective-permute-start.10
  636.4 4.5 collective-permute-start.11
  749.5 10.1 %collective-permute-start.12 = (f32[3,1,24,384]{3,2,1,0:T(8,128)S(1)}, f32[3,1,24,384]{3,2,1,0:T(8,128)S(1)}, u32[]{:S(2)}, u32[]{:S(2)}) collective-permute-start(f32[3,1,24,384]{3,2,1,0:T(8,128)S(1)} %slice.612), channel_id=1, source_target_pairs={{0,112},{16,0},{32,16},{48,32},{64,48},{80,64},{96,80},{112,96},{1... | collective-permute-start | bytes 331784 | tf_op jit(solution)/shard_map/ppermute | solution.py:19
  759.7 2.9 collective-permute-start.13
  878.7 6.5 copy-start.28
  878.8 6.0 collective-permute-start.14
  880.4 25.1 %copy-start.27 = (f32[27,1,8,128]{3,2,1,0:T(8,128)S(1)}, f32[27,1,8,128]{3,2,1,0:T(8,128)}, u32[]{:S(2)}) copy-start(f32[27,1,8,128]{3,2,1,0:T(8,128)} %param.10) | copy-start | bytes 331780
  880.4 57.5 %copy-start.23 = (f32[3,3,24,384]{3,2,1,0:T(8,128)S(1)}, f32[3,3,24,384]{3,2,1,0:T(8,128)}, u32[]{:S(2)}) copy-start(f32[3,3,24,384]{3,2,1,0:T(8,128)} %param.8) | copy-start | bytes 995332
  880.4 57.5 %copy-start.24 = (f32[3,3,24,384]{3,2,1,0:T(8,128)S(1)}, f32[3,3,24,384]{3,2,1,0:T(8,128)}, u32[]{:S(2)}) copy-start(f32[3,3,24,384]{3,2,1,0:T(8,128)} %param.9) | copy-start | bytes 995332
  884.9 2.9 collective-permute-start.15
  (20 other events, 48.2 us)
